TPU v7x, 256 devices: a whole 4x4x8 slice. The times are simulated.
256 devices in a mesh: mem: 64 (over z, x, core), lev: 4 (over y).
Axes of the slice: x: 4, y: 4, z: 8, core: 2. Of those that a mesh axis runs over, the one named last changes fastest.
Arguments:
- hx_ens: bfloat16 [128, 524288], P('mem', 'lev'), may hold values from -6 to 6
- obs_value: float32 [524288], P('lev'), may hold values from -6 to 6
- obs_error: float32 [524288], P('lev'), may hold values from 0.7 to 1.4
- obs_list: int32 [1024, 1024], P(None, 'lev'), may hold values from 0 to 131071, as said below
- obs_count: int32 [1024, 4], P(None, 'lev'), may hold values from 192 to 256, as said below
- loc_class: int32 [1024, 1024], P(None, 'lev'), may hold values from 0 to 2
- state: bfloat16 [128, 1024, 4096], P('mem', None, 'lev'), may hold values from -6 to 6
Outputs:
- increment: bfloat16 [128, 1024, 4096], P('mem', None, 'lev')
Inputs may be any that keep to these rules, and one draw needn't show every extreme that they name: `obs_list`: indices into the observations of the slot's level block, distinct within one patch's block of 256 slots; for patch p each index lies among the 384 indices that follow (p - 1) * 128 modulo 131072, that one included. `obs_count`: counts of the leading used slots; some patch and level block uses all 256 in every draw.
All inputs are finite; a program needn't handle non-finite values.
Results may differ from a plain program's by a relative error of at most 0.0076.
Values may be sent and summed in bfloat16 or wider, within the bound.
A program may use at most 128 MiB of HBM per device.

v0:
```python
import math

import jax
import jax.numpy as jnp
from jax import lax
from jax.sharding import PartitionSpec as P

ITERS = 6


highest = lax.Precision.HIGHEST


def inverse_root(matrix):
    size = matrix.shape[-1]
    identity = jnp.eye(size, dtype=jnp.float32)
    frob = jnp.sqrt(jnp.sum(matrix * matrix, axis=(-2, -1), keepdims=True))

    def sweep(index, carry):
        upper, lower = carry
        middle = 1.5 * identity - 0.5 * jnp.matmul(lower, upper, precision=highest)
        return (
            jnp.matmul(upper, middle, precision=highest),
            jnp.matmul(middle, lower, precision=highest),
        )

    start = (matrix / frob, jnp.broadcast_to(identity, matrix.shape))
    upper, lower = lax.fori_loop(0, ITERS, sweep, start)
    return lower / jnp.sqrt(frob)


def mixing(gram, pull):
    size = gram.shape[-1]
    identity = jnp.eye(size, dtype=jnp.float32)
    system = gram + (size - 1.0) * identity
    root = inverse_root(system)
    covar = jnp.matmul(root, root, precision=highest)
    centre = jnp.sum(covar * pull[..., None, :], axis=-1)
    weights = math.sqrt(size - 1.0) * root + centre[..., :, None] - identity
    return weights.astype(jnp.bfloat16)


def ensemble_products(received_rows):
    values = received_rows.astype(jnp.float32)
    average = jnp.mean(values, axis=0)
    spread = values - average[None]
    gram = jnp.einsum("apc,bpc->pab", spread, spread, precision=highest)
    pull = -jnp.einsum("apc,pc->pa", spread, average, precision=highest)
    return (gram, pull)


def apply_mixer(received_state, mixer):
    column = received_state.astype(jnp.float32)
    anomaly = (column - jnp.mean(column, axis=0)[None]).astype(jnp.bfloat16)
    return jnp.einsum("kpr,pkj->jpr", anomaly, mixer, preferred_element_type=jnp.float32).astype(
        jnp.bfloat16
    )


def select_slots(innov, obs_list):
    members, level_obs = innov.shape
    patches, capacity = obs_list.shape
    half = capacity // 2
    span = 3 * half
    blocks = innov.reshape(members, patches, half)
    window = jnp.concatenate(
        [jnp.roll(blocks, 1, axis=1), blocks, jnp.roll(blocks, -1, axis=1)], axis=2
    )
    anchor = (jnp.arange(patches, dtype=jnp.int32) - 1) * half
    offset = (obs_list - anchor[:, None]) % level_obs
    groups = 8
    group_size = patches // groups
    window_groups = jnp.transpose(window.reshape(members, groups, group_size, span), (1, 0, 2, 3))
    offset_groups = offset.reshape(groups, group_size, capacity)
    positions = jnp.arange(span, dtype=jnp.int32)

    def pick(pieces):
        values, where = pieces
        table = (positions[None, :, None] == where[:, None, :]).astype(jnp.float32)
        return jnp.einsum("kgw,gws->kgs", values, table, precision=highest)

    chosen = lax.map(pick, (window_groups, offset_groups))
    return jnp.transpose(chosen, (1, 0, 2, 3)).reshape(members, patches, capacity)


def body(hx_ens, obs_value, obs_error, obs_list, obs_count, loc_class, state):
    capacity = obs_list.shape[1]
    innov = (obs_value[None, :] - hx_ens.astype(jnp.float32)) / obs_error[None, :]
    picked = select_slots(innov, obs_list)
    in_use = jnp.arange(capacity, dtype=jnp.int32)[None, :] < obs_count
    weight = jnp.exp(-0.5 * (loc_class.astype(jnp.float32) / 3.0) ** 2) * in_use.astype(jnp.float32)
    innov_rows = (picked * weight[None]).astype(jnp.bfloat16)
    got_rows, got_state = (
        lax.all_to_all(innov_rows, "mem", split_axis=1, concat_axis=0, tiled=True),
        lax.all_to_all(state, "mem", split_axis=1, concat_axis=0, tiled=True),
    )
    gram_part, pull_part = ensemble_products(got_rows)
    gram, pull = lax.psum((gram_part, pull_part), "lev")
    mixer = mixing(gram, pull)
    result = apply_mixer(got_state, mixer)
    return lax.all_to_all(result, "mem", split_axis=0, concat_axis=1, tiled=True)


def solution(mesh):
    return jax.shard_map(
        body,
        mesh=mesh,
        in_specs=(
            P("mem", "lev"),
            P("lev"),
            P("lev"),
            P(None, "lev"),
            P(None, "lev"),
            P(None, "lev"),
            P("mem", None, "lev"),
        ),
        out_specs=P("mem", None, "lev"),
        check_vma=False,
    )
```

profile of v0, /device:TPU:1, one launch (start us, length us, event | category | flops | bytes accessed | tf_op | source)
XLA Modules:
  0.0 480.5 jit_solution(186623429222193283)
XLA Ops:
  10.1 2.7 add_select_fusion
  13.7 2.9 maximum_bitcast_fusion
  16.6 143.4 %while.24 = (s32[]{:T(128)}, f32[8,2,128,256]{3,1,2,0:T(2,128)S(1)}, s32[8,128,256]{2,1,0:T(8,128)}, f32[8,2,128,384]{3,1,2,0:T(2,128)}, s32[]{:T(128)}) while((s32[]{:T(128)}, f32[8,2,128,256]{3,1,2,0:T(2,128)S(1)}, s32[8,128,256]{2,1,0:T(8,128)}, f32[8,2,128,384]{3,1,2,0:T(2,128)}, s32[]{:T(128)}) %tuple.54), condition=%wide.region_1.2_spmd.clone, body=%wide.region_0.1_spmd.clone.sunk | while | flops 314572800 | bytes 1049673 | solution.py:82
  17.7 17.0 %fusion.55 = f32[8,2,128,256]{3,1,2,0:T(2,128)S(1)} fusion(f32[8,2,128,256]{3,1,2,0:T(2,128)S(1)} %get-tuple-element.157, s32[]{:T(128)S(6)} %copy.64, s32[128,256]{1,0:T(8,128)S(1)} %dynamic-slice_bitcast_fusion.2, f32[8,2,128,384]{3,1,2,0:T(2,128)} %get-tuple-element.164), kind=kOutput, calls=%fused_computation.6.clone.1 | convolution fusion | flops 314572800 | bytes 787456 | tf_op jit(solution)/shard_map/while/body/eval_jaxpr/kgw,gws->kgs/dot_general | solution.py:80
  35.6 17.0 %fusion.55 = f32[8,2,128,256]{3,1,2,0:T(2,128)S(1)} fusion(f32[8,2,128,256]{3,1,2,0:T(2,128)S(1)} %get-tuple-element.157, s32[]{:T(128)S(6)} %copy.64, s32[128,256]{1,0:T(8,128)S(1)} %dynamic-slice_bitcast_fusion.2, f32[8,2,128,384]{3,1,2,0:T(2,128)} %get-tuple-element.164), kind=kOutput, calls=%fused_computation.6.clone.1 | convolution fusion | flops 314572800 | bytes 787456 | tf_op jit(solution)/shard_map/while/body/eval_jaxpr/kgw,gws->kgs/dot_general | solution.py:80
  53.4 17.0 %fusion.55 = f32[8,2,128,256]{3,1,2,0:T(2,128)S(1)} fusion(f32[8,2,128,256]{3,1,2,0:T(2,128)S(1)} %get-tuple-element.157, s32[]{:T(128)S(6)} %copy.64, s32[128,256]{1,0:T(8,128)S(1)} %dynamic-slice_bitcast_fusion.2, f32[8,2,128,384]{3,1,2,0:T(2,128)} %get-tuple-element.164), kind=kOutput, calls=%fused_computation.6.clone.1 | convolution fusion | flops 314572800 | bytes 787456 | tf_op jit(solution)/shard_map/while/body/eval_jaxpr/kgw,gws->kgs/dot_general | solution.py:80
  71.3 17.0 %fusion.55 = f32[8,2,128,256]{3,1,2,0:T(2,128)S(1)} fusion(f32[8,2,128,256]{3,1,2,0:T(2,128)S(1)} %get-tuple-element.157, s32[]{:T(128)S(6)} %copy.64, s32[128,256]{1,0:T(8,128)S(1)} %dynamic-slice_bitcast_fusion.2, f32[8,2,128,384]{3,1,2,0:T(2,128)} %get-tuple-element.164), kind=kOutput, calls=%fused_computation.6.clone.1 | convolution fusion | flops 314572800 | bytes 787456 | tf_op jit(solution)/shard_map/while/body/eval_jaxpr/kgw,gws->kgs/dot_general | solution.py:80
  89.2 17.0 %fusion.55 = f32[8,2,128,256]{3,1,2,0:T(2,128)S(1)} fusion(f32[8,2,128,256]{3,1,2,0:T(2,128)S(1)} %get-tuple-element.157, s32[]{:T(128)S(6)} %copy.64, s32[128,256]{1,0:T(8,128)S(1)} %dynamic-slice_bitcast_fusion.2, f32[8,2,128,384]{3,1,2,0:T(2,128)} %get-tuple-element.164), kind=kOutput, calls=%fused_computation.6.clone.1 | convolution fusion | flops 314572800 | bytes 787456 | tf_op jit(solution)/shard_map/while/body/eval_jaxpr/kgw,gws->kgs/dot_general | solution.py:80
  107.1 17.0 %fusion.55 = f32[8,2,128,256]{3,1,2,0:T(2,128)S(1)} fusion(f32[8,2,128,256]{3,1,2,0:T(2,128)S(1)} %get-tuple-element.157, s32[]{:T(128)S(6)} %copy.64, s32[128,256]{1,0:T(8,128)S(1)} %dynamic-slice_bitcast_fusion.2, f32[8,2,128,384]{3,1,2,0:T(2,128)} %get-tuple-element.164), kind=kOutput, calls=%fused_computation.6.clone.1 | convolution fusion | flops 314572800 | bytes 787456 | tf_op jit(solution)/shard_map/while/body/eval_jaxpr/kgw,gws->kgs/dot_general | solution.py:80
  125.0 17.0 %fusion.55 = f32[8,2,128,256]{3,1,2,0:T(2,128)S(1)} fusion(f32[8,2,128,256]{3,1,2,0:T(2,128)S(1)} %get-tuple-element.157, s32[]{:T(128)S(6)} %copy.64, s32[128,256]{1,0:T(8,128)S(1)} %dynamic-slice_bitcast_fusion.2, f32[8,2,128,384]{3,1,2,0:T(2,128)} %get-tuple-element.164), kind=kOutput, calls=%fused_computation.6.clone.1 | convolution fusion | flops 314572800 | bytes 787456 | tf_op jit(solution)/shard_map/while/body/eval_jaxpr/kgw,gws->kgs/dot_general | solution.py:80
  142.9 17.0 %fusion.55 = f32[8,2,128,256]{3,1,2,0:T(2,128)S(1)} fusion(f32[8,2,128,256]{3,1,2,0:T(2,128)S(1)} %get-tuple-element.157, s32[]{:T(128)S(6)} %copy.64, s32[128,256]{1,0:T(8,128)S(1)} %dynamic-slice_bitcast_fusion.2, f32[8,2,128,384]{3,1,2,0:T(2,128)} %get-tuple-element.164), kind=kOutput, calls=%fused_computation.6.clone.1 | convolution fusion | flops 314572800 | bytes 787456 | tf_op jit(solution)/shard_map/while/body/eval_jaxpr/kgw,gws->kgs/dot_general | solution.py:80
  163.9 13.0 %all-to-all-start = ((bf16[2,1024,256]{2,0,1:T(2,128)(2,1)}), bf16[2,1024,256]{2,0,1:T(2,128)(2,1)S(1)}, u32[]{:S(2)}, u32[]{:S(2)}) async-start(bf16[2,1024,256]{2,0,1:T(2,128)(2,1)} %fusion.15), calls=%async_computation | async-start | bytes 2097152 | tf_op jit(solution)/shard_map/all_to_all | solution.py:94
  176.8 8.5 %copy.45 = bf16[2,1024,1024]{2,0,1:T(2,128)(2,1)} copy(bf16[2,1024,1024]{2,1,0:T(8,128)(2,1)} %param.17) | data formatting | bytes 8388608 | tf_op args[6]
  185.4 19.5 %all-to-all-done = bf16[2,1024,256]{2,0,1:T(2,128)(2,1)S(1)} async-done(((bf16[2,1024,256]{2,0,1:T(2,128)(2,1)}), bf16[2,1024,256]{2,0,1:T(2,128)(2,1)S(1)}, u32[]{:S(2)}, u32[]{:S(2)}) %all-to-all-start) | async-done | bytes 1048608 | tf_op jit(solution)/shard_map/all_to_all | solution.py:94
  204.8 6.7 %all-to-all-start.1 = ((bf16[2,1024,1024]{2,0,1:T(2,128)(2,1)}), bf16[2,1024,1024]{2,0,1:T(2,128)(2,1)}, u32[]{:S(2)}, u32[]{:S(2)}) async-start(bf16[2,1024,1024]{2,0,1:T(2,128)(2,1)} %copy.45), calls=%async_computation.1 | async-start | bytes 8388608 | tf_op jit(solution)/shard_map/all_to_all | solution.py:95
  211.9 3.0 convert_reduce_fusion.1
  215.1 2.4 copy_bitcast_fusion
  217.5 2.7 reshape.72
  220.2 3.2 fusion.18
  225.4 9.5 %psum.15 = f32[16,128]{1,0:T(8,128)S(1)} all-reduce(f32[16,128]{1,0:T(8,128)S(1)} %neg.3), channel_id=1, replica_groups=mesh['mem'=64,'lev'=4] {'lev'}, use_global_device_ids=true, to_apply=%region_8.9 | all-reduce | flops 2048 | bytes 16384 | tf_op jit(solution)/shard_map/psum | solution.py:98
  234.9 39.9 %all-reduce.2.cloned.1.call-done = f32[16,128,128]{2,1,0:T(8,128)} async-done(((f32[16,128,128]{2,1,0:T(8,128)}), f32[16,128,128]{2,1,0:T(8,128)}) %all-reduce.2.cloned.1.call-update) | async-done | bytes 1048592 | tf_op jit(solution)/shard_map/psum | solution.py:98
  278.1 34.0 %while.25 = (s32[]{:T(128)}, f32[16,128,128]{1,2,0:T(8,128)S(1)}, f32[16,128,128]{2,1,0:T(8,128)S(1)}, s32[]{:T(128)}) while((s32[]{:T(128)}, f32[16,128,128]{1,2,0:T(8,128)S(1)}, f32[16,128,128]{2,1,0:T(8,128)S(1)}, s32[]{:T(128)}) %tuple.48), condition=%wide.region_7.8_spmd.clone, body=%wide.region_6.7_spmd.clone.sunk | while | flops 1208516608 | bytes 13762613 | solution.py:28
  278.5 2.3 fusion.63
  295.4 2.3 fusion.63
  314.2 14.2 %convert_reduce_fusion = f32[1024,1024]{1,0:T(8,128)} fusion(bf16[2,1024,1024]{2,0,1:T(2,128)(2,1)} %all-to-all-done.1), kind=kLoop, calls=%fused_computation.24 | loop fusion | flops 3145728 | bytes 8388608 | tf_op jit(solution)/shard_map/reduce_sum | solution.py:54
  328.4 2.4 reduce_sum.57
  330.8 8.3 %convert_element_type.92 = f32[2,1024,1024]{2,0,1:T(2,128)} convert(bf16[2,1024,1024]{2,0,1:T(2,128)(2,1)} %all-to-all-done.1) | non-fusion elementwise | flops 2097152 | bytes 12582912 | tf_op jit(solution)/shard_map/convert_element_type | solution.py:53
  339.1 7.6 %copy.46 = f32[64,2,16,1024]{3,1,0,2:T(2,128)} copy(f32[64,2,16,1024]{3,1,2,0:T(2,128)} %bitcast.80) | data formatting | bytes 16777216 | tf_op jit(solution)/shard_map/convert_element_type | solution.py:53
  346.7 10.9 %reshape.73 = f32[128,16,1024]{2,0,1:T(8,128)} reshape(f32[64,2,16,1024]{3,1,0,2:T(2,128)} %copy.46) | data formatting | bytes 16777216 | tf_op jit(solution)/shard_map/convert_element_type | solution.py:53
  357.6 4.9 %convert_bitcast_fusion = bf16[128,16,1024]{2,0,1:T(8,128)(2,1)S(1)} fusion(f32[128,16,1024]{2,0,1:T(8,128)} %reshape.73, f32[16,1024]{1,0:T(8,128)S(1)} %broadcast_multiply_fusion, f32[16,128]{1,0:T(8,128)S(1)} %fusion.20, f32[128,128]{1,0:T(8,128)S(1)} %fusion.27, f32[16,128,128]{2,1,0:T(8,128)S(1)} %get-tuple-element.55, f32[16]{0:T(128)S(1)} %get-tuple-element.103), kind=kOutput, calls=%fused_computation.18 | convolution fusion | flops 544473088 | bytes 13770816 | tf_op jit(solution)/shard_map/kpr,pkj->jpr/dot_general | solution.py:55
  364.8 106.2 %all_to_all.36 = bf16[128,16,1024]{2,1,0:T(8,128)(2,1)S(1)} all-to-all(bf16[128,16,1024]{2,1,0:T(8,128)(2,1)S(1)} %copy.48), channel_id=1, replica_groups=mesh['mem'=64,'lev'=4] {'mem'}, dimensions={0} | all-to-all | bytes 8388608 | tf_op jit(solution)/shard_map/all_to_all | solution.py:101
  471.0 2.5 copy.49
  (78 shorter events, 54.6 us)
Async XLA Ops:
  6.5 2.8 copy-start
  6.5 2.8 copy-start.1
  6.5 2.8 copy-start.2
  13.7 2.9 copy-start.3
  16.6 143.4 %copy-start.4 = (s32[1024,1]{0,1:T(1,128)S(1)}, s32[1024,1]{0,1:T(1,128)}, u32[]{:S(2)}) copy-start(s32[1024,1]{0,1:T(1,128)} %param.15) | copy-start | bytes 12292
  163.9 41.0 %all-to-all-start = ((bf16[2,1024,256]{2,0,1:T(2,128)(2,1)}), bf16[2,1024,256]{2,0,1:T(2,128)(2,1)S(1)}, u32[]{:S(2)}, u32[]{:S(2)}) async-start(bf16[2,1024,256]{2,0,1:T(2,128)(2,1)} %fusion.15), calls=%async_computation | async-start | bytes 2097152 | tf_op jit(solution)/shard_map/all_to_all | solution.py:94
  204.8 109.4 %all-to-all-start.1 = ((bf16[2,1024,1024]{2,0,1:T(2,128)(2,1)}), bf16[2,1024,1024]{2,0,1:T(2,128)(2,1)}, u32[]{:S(2)}, u32[]{:S(2)}) async-start(bf16[2,1024,1024]{2,0,1:T(2,128)(2,1)} %copy.45), calls=%async_computation.1 | async-start | bytes 8388608 | tf_op jit(solution)/shard_map/all_to_all | solution.py:95
  211.5 63.3 %all-reduce.2.cloned.1.call-start = ((), (), s32[]{:S(2)}) async-start(), calls=%async_computation.3 | async-start | bytes 2097152 | tf_op jit(solution)/shard_map/psum | solution.py:98
Sparse Core Ops, SparseCore 0:
  223.6 51.2 all-reduce.1
where the time goes:
time: 486 us; the launch traced here: 481 us
  matrix products  180 us (37%)
  blocking collectives  116 us (24%)
  waiting for transfers between devices  59.4 us (12%)
  other arithmetic  46.6 us (10%)
  local copies, waits for them, and re-layouts  43.6 us (9%)
  starting transfers between devices  20.1 us (4%)
  between operations  13.8 us (3%)
    dot_general x8, matrix products, pick(): return jnp.einsum('kgw,gws->kgs', values, table, precision=highest)  136 us
    all_to_all x1, blocking collectives, body(): lax.all_to_all(result, 'mem', split_axis=0, concat_axis=1, tiled=True)  106 us
    psum x1, waiting for transfers between devices, body(): gram, pull = lax.psum((gram_part, pull_part), 'lev')  39.9 us
    all_to_all x1, waiting for transfers between devices, body(): lax.all_to_all(innov_rows, 'mem', split_axis=1, concat_axis=0, tiled=True)  19.5 us
    convert_element_type x2, local copies, waits for them, and re-layouts, apply_mixer(): column = received_state.astype(jnp.float32)  18.5 us
    reduce_sum x2, other arithmetic, apply_mixer(): anomaly = (column - jnp.mean(column, axis=0)[None]).astype(jnp.bfloat16)  16.6 us
    dot_general x6, matrix products, sweep(): middle = 1.5 * identity - 0.5 * jnp.matmul(lower, upper, precision=highest)  14 us
    all_to_all x1, starting transfers between devices, body(): lax.all_to_all(innov_rows, 'mem', split_axis=1, concat_axis=0, tiled=True)  13 us
  transfers between devices with their start and end apart: 3, of which 2 were waited for; matrix products, arithmetic and copies ran while one was open for 13% of the time, Pallas kernels for 0%

commit v1 on v0

v1 whole, which is shorter than its diff:
```python
import functools
import math

import jax
import jax.numpy as jnp
from jax import lax
from jax.experimental import pallas as pl
from jax.experimental.pallas import tpu as pltpu
from jax.sharding import PartitionSpec as P

ITERS = 6
MEMBERS = 128
GROUP = 64
LEVS = 4
PER = 16
QUART = PER // LEVS
HALF = 128
CAPACITY = 256
LEVEL_OBS = 131072
COLUMNS = 1024
CHUNKS = 4
WIDE = COLUMNS // CHUNKS
TILES = WIDE // 128
GRAM_ROWS = MEMBERS + 8

MESH = pl.DeviceIdType.MESH
HIGHEST = lax.Precision.HIGHEST
f32 = jnp.float32
bf16 = jnp.bfloat16


def dot_nt(a, b, precision=None):
    return lax.dot_general(
        a, b, (((1,), (1,)), ((), ())), precision=precision, preferred_element_type=f32
    )


def dot_nn(a, b, precision=None):
    return jnp.dot(a, b, precision=precision, preferred_element_type=f32)


def kernel(
    hx_ref, value_ref, error_ref, list_ref, count_ref, class_ref, state_ref,
    out_ref,
    hx_in, hx_rows, hx_win, obs_in, pieces, slot_in, count_in, weight,
    gram_out, gram_in, upper, lower, mixers,
    state_in, anomaly, product, result,
    hx_send, hx_recv, halo_send, halo_recv, local_sem,
    gram_send, gram_recv, mix_send, mix_recv,
    state_send, state_recv, out_send, out_recv,
):
    me = lax.axis_index("mem")
    lev = lax.axis_index("lev")
    depth, low = me // 8, me % 8
    before, after = (me + GROUP - 1) % GROUP, (me + 1) % GROUP

    barrier = pltpu.get_barrier_semaphore()

    @pl.loop(1, GROUP)
    def _(i):
        pl.semaphore_signal(barrier, inc=1, device_id=((me + i) % GROUP, lev), device_id_type=MESH)

    for i in range(1, LEVS):
        pl.semaphore_signal(barrier, inc=1, device_id=(me, (lev + i) % LEVS), device_id_type=MESH)

    local = []
    for k, source in enumerate((value_ref, error_ref)):
        for j, block in enumerate((before, me, after)):
            local.append(
                pltpu.make_async_copy(
                    source.at[pl.ds(block * PER, PER)], obs_in.at[k, pl.ds(j * PER, PER)],
                    local_sem.at[k * 3 + j],
                )
            )
    for k, source in enumerate((list_ref, class_ref)):
        local.append(
            pltpu.make_async_copy(source.at[pl.ds(me * PER, PER)], slot_in.at[k], local_sem.at[6 + k])
        )
    local.append(pltpu.make_async_copy(count_ref, count_in, local_sem.at[8]))
    for copy in local:
        copy.start()
    pltpu.make_async_copy(
        hx_ref.at[:, pl.ds(me * PER, PER)], hx_in.at[pl.ds(me * 2, 2)], hx_recv
    ).start()
    for q in range(CHUNKS):
        cols = pl.ds(q * WIDE, WIDE)
        pltpu.make_async_copy(
            state_ref.at[:, pl.ds(me * PER, PER), cols], state_in.at[q, pl.ds(me * 2, 2)], state_recv.at[q]
        ).start()

    pl.semaphore_wait(barrier, GROUP - 1 + LEVS - 1)

    def to_all(send):
        @pl.loop(0, 8)
        def _(j):
            for dz in (4, 1, 7, 2, 6, 3, 5, 0):
                target = ((depth + dz) % 8) * 8 + (low + j) % 8
                if dz == 0:

                    @pl.when(j > 0)
                    def _():
                        send(target)
                else:
                    send(target)

    def send_hx(target):
        pltpu.make_async_remote_copy(
            src_ref=hx_ref.at[:, pl.ds(target * PER, PER)],
            dst_ref=hx_in.at[pl.ds(me * 2, 2)],
            send_sem=hx_send, recv_sem=hx_recv, device_id=(target, lev), device_id_type=MESH,
        ).start()

    to_all(send_hx)

    for q in range(CHUNKS):

        def send_state(target, q=q):
            pltpu.make_async_remote_copy(
                src_ref=state_ref.at[:, pl.ds(target * PER, PER), pl.ds(q * WIDE, WIDE)],
                dst_ref=state_in.at[q, pl.ds(me * 2, 2)],
                send_sem=state_send, recv_sem=state_recv.at[q],
                device_id=(target, lev), device_id_type=MESH,
            ).start()

        to_all(send_state)

    for copy in local:
        copy.wait()
    lanes = lax.broadcasted_iota(jnp.int32, (8, 128), 1)
    rows8 = lax.broadcasted_iota(jnp.int32, (8, 128), 0)
    mine = jnp.sum(jnp.where(rows8 == me // 8, count_in[...], 0), axis=0, keepdims=True)
    spots = lax.broadcasted_iota(jnp.int32, (PER, 128), 1) - (me % 8) * PER
    patch_rows = lax.broadcasted_iota(jnp.int32, (PER, 128), 0)
    counts = jnp.sum(jnp.where(spots == patch_rows, mine, 0), axis=1, keepdims=True)
    slots = lax.broadcasted_iota(jnp.int32, (PER, CAPACITY), 1)
    scaled = slot_in[1].astype(f32) / 3.0
    weight[...] = jnp.where(slots < counts, jnp.exp(-0.5 * (scaled * scaled)), 0.0)
    del lanes
    for k in range(2):
        rest = obs_in[k]
        for j in range(3):
            piece = rest.astype(bf16).astype(f32)
            pieces[k * 3 + j] = piece
            rest = rest - piece

    pltpu.make_async_copy(hx_in, hx_in, hx_recv).wait()
    hx_rows[...] = hx_in[...].astype(f32).reshape(MEMBERS * PER, 128)

    def take_block(b):
        hx_win[b + 1] = hx_rows[pl.ds(b, MEMBERS, stride=PER), :].astype(bf16)

    for b in range(PER):
        take_block(b)
    halo = [
        pltpu.make_async_remote_copy(
            src_ref=hx_win.at[1], dst_ref=hx_win.at[PER + 1],
            send_sem=halo_send.at[0], recv_sem=halo_recv.at[0],
            device_id=(before, lev), device_id_type=MESH,
        ),
        pltpu.make_async_remote_copy(
            src_ref=hx_win.at[PER], dst_ref=hx_win.at[0],
            send_sem=halo_send.at[1], recv_sem=halo_recv.at[1],
            device_id=(after, lev), device_id_type=MESH,
        ),
    ]
    for copy in halo:
        copy.start()

    def patch_gram(p):
        anchor = (me * PER + p - 1) * HALF
        offset = (slot_in[0, pl.ds(p, 1), :] - anchor) & (LEVEL_OBS - 1)
        places = lax.broadcasted_iota(jnp.int32, (HALF, CAPACITY), 0)
        chosen = jnp.zeros((MEMBERS, CAPACITY), f32)
        observed = jnp.zeros((8, CAPACITY), f32)
        for j in range(3):
            table = jnp.where(places + j * HALF == offset, 1.0, 0.0).astype(bf16)
            chosen += dot_nn(hx_win[p + j], table)
            parts = [pieces[k, pl.ds(PER - 1 + p + j, 1), :] for k in range(6)]
            stack = jnp.concatenate(parts + [jnp.zeros((2, HALF), f32)], axis=0)
            observed += dot_nn(stack.astype(bf16), table)
        value = observed[0:1] + observed[1:2] + observed[2:3]
        error = observed[3:4] + observed[4:5] + observed[5:6]
        innov = ((value - chosen) / error * weight[pl.ds(p, 1), :]).astype(bf16).astype(f32)
        average = jnp.mean(innov, axis=0, keepdims=True)
        spread = innov - average
        both = jnp.concatenate([spread, jnp.broadcast_to(average, (8, CAPACITY))], axis=0)
        gram_out[p] = dot_nt(both, spread, HIGHEST)

    @pl.loop(1, PER - 1)
    def _(p):
        patch_gram(p)

    for copy in halo:
        copy.wait()

    @pl.loop(0, 2)
    def _(i):
        patch_gram(i * (PER - 1))

    gram_copies = []
    for i in range(1, LEVS):
        target = (lev + i) % LEVS
        gram_copies.append(
            pltpu.make_async_remote_copy(
                src_ref=gram_out.at[pl.ds(target * QUART, QUART)],
                dst_ref=gram_in.at[i - 1],
                send_sem=gram_send.at[i - 1], recv_sem=gram_recv.at[i - 1],
                device_id=(me, target), device_id_type=MESH,
            )
        )
    for copy in gram_copies:
        copy.start()
    for copy in gram_copies:
        copy.wait()

    diagonal = lax.broadcasted_iota(jnp.int32, (MEMBERS, MEMBERS), 0) == lax.broadcasted_iota(
        jnp.int32, (MEMBERS, MEMBERS), 1
    )
    identity = jnp.where(diagonal, 1.0, 0.0).astype(f32)
    frobs, pulls = [], []
    for k in range(QUART):
        total = gram_out[lev * QUART + k] + gram_in[0, k] + gram_in[1, k] + gram_in[2, k]
        system = total[:MEMBERS] + (MEMBERS - 1.0) * identity
        squares = jnp.sum(jnp.sum(system * system, axis=0, keepdims=True), axis=1, keepdims=True)
        frob = jnp.sqrt(squares)
        frobs.append(frob)
        pulls.append(-total[MEMBERS : MEMBERS + 1])
        upper[k] = system / frob
        lower[k] = identity

    @pl.loop(0, ITERS)
    def _(step):
        middles = [
            1.5 * identity - 0.5 * dot_nn(lower[k], upper[k], HIGHEST) for k in range(QUART)
        ]
        uppers = [dot_nn(upper[k], middles[k], HIGHEST) for k in range(QUART)]
        lowers = [dot_nn(middles[k], lower[k], HIGHEST) for k in range(QUART)]
        for k in range(QUART):
            upper[k] = uppers[k]
            lower[k] = lowers[k]

    for k in range(QUART):
        root = lower[k] / jnp.sqrt(frobs[k])
        covar = dot_nn(root, root, HIGHEST)
        centre = jnp.sum(covar * pulls[k], axis=1, keepdims=True)
        mixer = math.sqrt(MEMBERS - 1.0) * root + centre - identity
        mixers[lev * QUART + k] = mixer.T.astype(bf16)

    mix_copies = []
    for i in range(1, LEVS):
        target = (lev + i) % LEVS
        mix_copies.append(
            pltpu.make_async_remote_copy(
                src_ref=mixers.at[pl.ds(lev * QUART, QUART)],
                dst_ref=mixers.at[pl.ds(lev * QUART, QUART)],
                send_sem=mix_send.at[i - 1], recv_sem=mix_recv.at[i - 1],
                device_id=(me, target), device_id_type=MESH,
            )
        )
    for copy in mix_copies:
        copy.start()
    for copy in mix_copies:
        copy.wait()

    for q in range(CHUNKS):
        cols = pl.ds(q * WIDE, WIDE)
        pltpu.make_async_copy(state_in.at[q], state_in.at[q], state_recv.at[q]).wait()
        for t in range(TILES):
            tile = slice(t * 128, (t + 1) * 128)

            def add(i, total):
                block = state_in[q, pl.ds(i * 8, 8), :, tile].astype(f32)
                return total + jnp.sum(block, axis=0)

            total = lax.fori_loop(0, MEMBERS // 8, add, jnp.zeros((PER, 128), f32))
            mean = total / MEMBERS

            @pl.loop(0, MEMBERS // 8)
            def _(i):
                block = state_in[q, pl.ds(i * 8, 8), :, tile].astype(f32) - mean[None]
                anomaly[t, pl.ds(i * 8 * PER, 8 * PER), :] = block.reshape(8 * PER, 128)

        for p in range(PER):
            right = jnp.concatenate(
                [anomaly[t, pl.ds(p, MEMBERS, stride=PER), :] for t in range(TILES)], axis=1
            ).astype(bf16)
            left = dot_nn(mixers[p], right)
            for t in range(TILES):
                product[t, pl.ds(p, MEMBERS, stride=PER), :] = left[:, t * 128 : (t + 1) * 128]

        for t in range(TILES):
            tile = slice(t * 128, (t + 1) * 128)

            @pl.loop(0, MEMBERS // 8)
            def _(i):
                block = product[t, pl.ds(i * 8 * PER, 8 * PER), :]
                result[q, pl.ds(i * 8, 8), :, tile] = block.reshape(8, PER, 128).astype(bf16)

        pltpu.make_async_copy(
            result.at[q, pl.ds(me * 2, 2)], out_ref.at[:, pl.ds(me * PER, PER), cols], out_recv
        ).start()

        def send_result(target, q=q, cols=cols):
            pltpu.make_async_remote_copy(
                src_ref=result.at[q, pl.ds(target * 2, 2)],
                dst_ref=out_ref.at[:, pl.ds(me * PER, PER), cols],
                send_sem=out_send, recv_sem=out_recv,
                device_id=(target, lev), device_id_type=MESH,
            ).start()

        to_all(send_result)

    others = GROUP - 1
    pltpu.make_async_copy(
        hx_in.at[pl.ds(0, 2 * others)], hx_in.at[pl.ds(0, 2 * others)], hx_send
    ).wait()
    sent = state_ref.at[:, pl.ds(0, PER * others)]
    pltpu.make_async_copy(sent, sent, state_send).wait()
    pltpu.make_async_copy(sent, sent, out_send).wait()
    pltpu.make_async_copy(out_ref, out_ref, out_recv).wait()


def body(hx_ens, obs_value, obs_error, obs_list, obs_count, loc_class, state):
    blocks = LEVEL_OBS // HALF
    dma = pltpu.SemaphoreType.DMA
    any_space = pl.BlockSpec(memory_space=pl.ANY)
    return pl.pallas_call(
        kernel,
        out_shape=jax.ShapeDtypeStruct(state.shape, bf16),
        in_specs=[any_space] * 7,
        out_specs=any_space,
        scratch_shapes=[
            pltpu.VMEM((MEMBERS, PER, 128), bf16),
            pltpu.VMEM((MEMBERS * PER, 128), f32),
            pltpu.VMEM((PER + 2, MEMBERS, 128), bf16),
            pltpu.VMEM((2, 3 * PER, 128), f32),
            pltpu.VMEM((6, 3 * PER, 128), f32),
            pltpu.VMEM((2, PER, CAPACITY), jnp.int32),
            pltpu.VMEM((8, 128), jnp.int32),
            pltpu.VMEM((PER, CAPACITY), f32),
            pltpu.VMEM((PER, GRAM_ROWS, MEMBERS), f32),
            pltpu.VMEM((LEVS - 1, QUART, GRAM_ROWS, MEMBERS), f32),
            pltpu.VMEM((QUART, MEMBERS, MEMBERS), f32),
            pltpu.VMEM((QUART, MEMBERS, MEMBERS), f32),
            pltpu.VMEM((PER, MEMBERS, MEMBERS), bf16),
            pltpu.VMEM((CHUNKS, MEMBERS, PER, WIDE), bf16),
            pltpu.VMEM((TILES, MEMBERS * PER, 128), f32),
            pltpu.VMEM((TILES, MEMBERS * PER, 128), f32),
            pltpu.VMEM((CHUNKS, MEMBERS, PER, WIDE), bf16),
            dma, dma, dma((2,)), dma((2,)), dma((9,)),
            dma((3,)), dma((3,)), dma((3,)), dma((3,)),
            dma, dma((CHUNKS,)), dma, dma,
        ],
        compiler_params=pltpu.CompilerParams(
            collective_id=0, has_side_effects=True, vmem_limit_bytes=48 << 20
        ),
        cost_estimate=pl.CostEstimate(flops=2_000_000_000, bytes_accessed=20_000_000, transcendentals=0),
    )(
        hx_ens.reshape(2, blocks, HALF),
        obs_value.reshape(blocks, HALF),
        obs_error.reshape(blocks, HALF),
        obs_list,
        obs_count.reshape(8, 128),
        loc_class,
        state,
    )


def solution(mesh):
    return jax.shard_map(
        body,
        mesh=mesh,
        in_specs=(
            P("mem", "lev"),
            P("lev"),
            P("lev"),
            P(None, "lev"),
            P(None, "lev"),
            P(None, "lev"),
            P("mem", None, "lev"),
        ),
        out_specs=P("mem", None, "lev"),
        check_vma=False,
    )
```

time: 486 us -> 216 us (0.44); the launches traced: 481 us -> 216 us
  Pallas kernels: 0 us -> 205 us
  matrix products: 180 us -> 0 us
  blocking collectives: 116 us -> 0 us
  waiting for transfers between devices: 59.4 us -> 0 us
  other arithmetic: 46.6 us -> 0 us
  local copies, waits for them, and re-layouts: 43.6 us -> 11 us
  starting transfers between devices: 20.1 us -> 0 us
  between operations: 13.8 us -> 0.02 us
    pallas_call x0 -> x1, Pallas kernels: none -> 205 us  [body(): pl.pallas_call(kernel, out_shape=jax.ShapeDtypeStruct(state.shape, bf16),...]
    dot_general x30 -> x0, matrix products: 180 us -> none  [the longest x8 136 us: pick(): return jnp.einsum('kgw,gws->kgs', values, table, precision=highest)]
    all_to_all x1 -> x0, blocking collectives: 106 us -> none  [body(): lax.all_to_all(result, 'mem', split_axis=0, concat_axis=1, tiled=True)]
    psum x1 -> x0, waiting for transfers between devices: 39.9 us -> none  [body(): gram, pull = lax.psum((gram_part, pull_part), 'lev')]
    convert_element_type x4 -> x0, local copies, waits for them, and re-layouts: 23.5 us -> none  [the longest x2 18.5 us: apply_mixer(): column = received_state.astype(jnp.float32)]
    reduce_sum x5 -> x0, other arithmetic: 21.1 us -> none  [the longest x2 16.6 us: apply_mixer(): anomaly = (column - jnp.mean(column, axis=0)[None]).astype(jnp.bfloat16)]
    all_to_all x2 -> x0, starting transfers between devices: 19.6 us -> none  [the longest x1 13 us: body(): lax.all_to_all(innov_rows, 'mem', split_axis=1, concat_axis=0, tiled=True)]
    all_to_all x2 -> x0, waiting for transfers between devices: 19.5 us -> none  [the longest x1 19.5 us: body(): lax.all_to_all(innov_rows, 'mem', split_axis=1, concat_axis=0, tiled=True)]
  transfers between devices with their start and end apart: 3 -> 0, of which waited for: 2 -> 0; matrix products, arithmetic and copies ran while one was open for 13% -> 0% of each run, Pallas kernels for 0% -> 0%
where the time goes in v1:
time: 216 us
  Pallas kernels  205 us (95%)
  local copies, waits for them, and re-layouts  11 us (5%)
    pallas_call x1, Pallas kernels, body(): pl.pallas_call(kernel, out_shape=jax.ShapeDtypeStruct(state.shape, bf16),...  205 us
    unnamed x12, local copies, waits for them, and re-layouts  11 us

profile of v1, /device:TPU:1, one launch (start us, length us, event | category | flops | bytes accessed | tf_op | source)
XLA Modules:
  0.0 215.9 jit_solution(7889322515447003016)
XLA Ops:
  0.0 1.1 copy.10
  1.1 0.0 copy-start
  1.1 1.2 copy-done
  2.3 0.0 copy-start.1
  2.3 1.2 copy-done.1
  3.6 0.0 copy-start.2
  3.6 1.0 copy-done.2
  4.6 0.0 copy-start.3
  4.6 1.0 copy-done.3
  5.7 0.0 copy-start.4
  5.7 0.7 copy-done.4
  6.3 204.9 %shard_map.73 = bf16[2,1024,1024]{2,1,0:T(8,128)(2,1)} custom-call(bf16[2,1024,128]{2,1,0:T(8,128)(2,1)S(1)} %bitcast.7, f32[1024,128]{1,0:T(8,128)S(1)} %bitcast.8, f32[1024,128]{1,0:T(8,128)S(1)} %bitcast.9, s32[1024,256]{1,0:T(8,128)S(1)} %copy-done, s32[8,128]{1,0:T(8,128)S(1)} %bitcast.10, s32[1024,256]{1,0:T(8,128)S(1)} %copy-done.1, ...), custom_call_target="tpu_custom_call" | custom-call | flops 2000000000 | bytes 20000000 | tf_op jit(solution)/shard_map/pallas_call | solution.py:327
  211.2 4.6 %copy.12 = bf16[2,1024,1024]{2,1,0:T(8,128)(2,1)} copy(bf16[2,1024,1024]{2,1,0:T(8,128)(2,1)} %shard_map.73) | data formatting | bytes 8388608
Async XLA Ops:
  1.1 1.2 copy-start
  2.3 1.2 copy-start.1
  3.6 1.0 copy-start.2
  4.6 1.0 copy-start.3
  5.7 0.7 copy-start.4

commit v2 on v1

--- a/solution.py
+++ b/solution.py
@@ -323,12 +323,12 @@
 def body(hx_ens, obs_value, obs_error, obs_list, obs_count, loc_class, state):
     blocks = LEVEL_OBS // HALF
     dma = pltpu.SemaphoreType.DMA
-    any_space = pl.BlockSpec(memory_space=pl.ANY)
+    any_space = pl.BlockSpec(memory_space=pltpu.HBM)
     return pl.pallas_call(
         kernel,
-        out_shape=jax.ShapeDtypeStruct(state.shape, bf16),
+        out_shape=pltpu.VMEM(state.shape, bf16),
         in_specs=[any_space] * 7,
-        out_specs=any_space,
+        out_specs=pl.BlockSpec(memory_space=pltpu.VMEM),
         scratch_shapes=[
             pltpu.VMEM((MEMBERS, PER, 128), bf16),
             pltpu.VMEM((MEMBERS * PER, 128), f32),
@@ -352,17 +352,22 @@
             dma, dma((CHUNKS,)), dma, dma,
         ],
         compiler_params=pltpu.CompilerParams(
-            collective_id=0, has_side_effects=True, vmem_limit_bytes=48 << 20
+            collective_id=0, has_side_effects=True, vmem_limit_bytes=40 << 20
         ),
         cost_estimate=pl.CostEstimate(flops=2_000_000_000, bytes_accessed=20_000_000, transcendentals=0),
     )(
-        hx_ens.reshape(2, blocks, HALF),
-        obs_value.reshape(blocks, HALF),
-        obs_error.reshape(blocks, HALF),
-        obs_list,
-        obs_count.reshape(8, 128),
-        loc_class,
-        state,
+        *(
+            pltpu.with_memory_space_constraint(operand, pltpu.HBM)
+            for operand in (
+                hx_ens.reshape(2, blocks, HALF),
+                obs_value.reshape(blocks, HALF),
+                obs_error.reshape(blocks, HALF),
+                obs_list,
+                obs_count.reshape(8, 128),
+                loc_class,
+                state,
+            )
+        )
     )
 
 

time: 216 us -> 209 us (0.968)
  local copies, waits for them, and re-layouts: 11 us -> 3.92 us
    unnamed x12 -> x2, local copies, waits for them, and re-layouts: 11 us -> 3.92 us
where the time goes in v2:
time: 209 us
  Pallas kernels  205 us (98%)
  local copies, waits for them, and re-layouts  3.92 us (2%)
    pallas_call x1, Pallas kernels, body(): pl.pallas_call(kernel, out_shape=pltpu.VMEM(state.shape, bf16), in_specs=...  205 us

profile of v2, /device:TPU:1, one launch (start us, length us, event | category | flops | bytes accessed | tf_op | source)
XLA Modules:
  0.0 208.9 jit_solution(4863373145350948818)
XLA Ops:
  0.0 1.9 copy.10
  1.9 205.0 %shard_map.73 = bf16[2,1024,1024]{2,1,0:T(8,128)(2,1)S(1)} custom-call(bf16[2,1024,128]{2,1,0:T(8,128)(2,1)} %bitcast.7, f32[1024,128]{1,0:T(8,128)} %bitcast.8, f32[1024,128]{1,0:T(8,128)} %bitcast.9, s32[1024,256]{1,0:T(8,128)} %list_ref.1, s32[8,128]{1,0:T(8,128)} %bitcast.11, s32[1024,256]{1,0:T(8,128)} %class_ref.1, bf16[2,1024,1024]{2,1,0:T(8,128)(2,1)} %state_ref.1), custom_call_target="tpu_custom_call" | custom-call | flops 2000000000 | bytes 20000000 | tf_op jit(solution)/shard_map/pallas_call | solution.py:327
  206.9 2.0 copy.12

commit v3 on v2

--- a/solution.py
+++ b/solution.py
@@ -42,7 +42,7 @@
 def kernel(
     hx_ref, value_ref, error_ref, list_ref, count_ref, class_ref, state_ref,
     out_ref,
-    hx_in, hx_rows, hx_win, obs_in, pieces, slot_in, count_in, weight,
+    hx_in, hx_win, obs_in, pieces, slot_in, count_in, weight,
     gram_out, gram_in, upper, lower, mixers,
     state_in, anomaly, product, result,
     hx_send, hx_recv, halo_send, halo_recv, local_sem,
@@ -80,7 +80,7 @@
     for copy in local:
         copy.start()
     pltpu.make_async_copy(
-        hx_ref.at[:, pl.ds(me * PER, PER)], hx_in.at[pl.ds(me * 2, 2)], hx_recv
+        hx_ref.at[pl.ds(me * PER, PER)], hx_in.at[me], hx_recv
     ).start()
     for q in range(CHUNKS):
         cols = pl.ds(q * WIDE, WIDE)
@@ -105,8 +105,8 @@
 
     def send_hx(target):
         pltpu.make_async_remote_copy(
-            src_ref=hx_ref.at[:, pl.ds(target * PER, PER)],
-            dst_ref=hx_in.at[pl.ds(me * 2, 2)],
+            src_ref=hx_ref.at[pl.ds(target * PER, PER)],
+            dst_ref=hx_in.at[me],
             send_sem=hx_send, recv_sem=hx_recv, device_id=(target, lev), device_id_type=MESH,
         ).start()
 
@@ -144,10 +144,9 @@
             rest = rest - piece
 
     pltpu.make_async_copy(hx_in, hx_in, hx_recv).wait()
-    hx_rows[...] = hx_in[...].astype(f32).reshape(MEMBERS * PER, 128)
 
     def take_block(b):
-        hx_win[b + 1] = hx_rows[pl.ds(b, MEMBERS, stride=PER), :].astype(bf16)
+        hx_win[b + 1] = hx_in[:, b].astype(f32).reshape(MEMBERS, 128).astype(bf16)
 
     for b in range(PER):
         take_block(b)
@@ -312,7 +311,7 @@
 
     others = GROUP - 1
     pltpu.make_async_copy(
-        hx_in.at[pl.ds(0, 2 * others)], hx_in.at[pl.ds(0, 2 * others)], hx_send
+        hx_in.at[pl.ds(0, others)], hx_in.at[pl.ds(0, others)], hx_send
     ).wait()
     sent = state_ref.at[:, pl.ds(0, PER * others)]
     pltpu.make_async_copy(sent, sent, state_send).wait()
@@ -330,8 +329,7 @@
         in_specs=[any_space] * 7,
         out_specs=pl.BlockSpec(memory_space=pltpu.VMEM),
         scratch_shapes=[
-            pltpu.VMEM((MEMBERS, PER, 128), bf16),
-            pltpu.VMEM((MEMBERS * PER, 128), f32),
+            pltpu.VMEM((GROUP, PER, 2, 128), bf16),
             pltpu.VMEM((PER + 2, MEMBERS, 128), bf16),
             pltpu.VMEM((2, 3 * PER, 128), f32),
             pltpu.VMEM((6, 3 * PER, 128), f32),
@@ -359,7 +357,7 @@
         *(
             pltpu.with_memory_space_constraint(operand, pltpu.HBM)
             for operand in (
-                hx_ens.reshape(2, blocks, HALF),
+                hx_ens.reshape(2, blocks, HALF).transpose(1, 0, 2),
                 obs_value.reshape(blocks, HALF),
                 obs_error.reshape(blocks, HALF),
                 obs_list,

time: 209 us -> 207 us (level)
  no operation moved by 1% of the time
where the time goes in v3:
time: 207 us
  Pallas kernels  205 us (99%)
    pallas_call x1, Pallas kernels, body(): pl.pallas_call(kernel, out_shape=pltpu.VMEM(state.shape, bf16), in_specs=...  205 us

profile of v3, /device:TPU:1, one launch (start us, length us, event | category | flops | bytes accessed | tf_op | source)
XLA Modules:
  0.0 207.1 jit_solution(11032451150524089976)
XLA Ops:
  0.0 205.1 %shard_map.73 = bf16[2,1024,1024]{2,1,0:T(8,128)(2,1)S(1)} custom-call(bf16[1024,2,128]{2,1,0:T(2,128)(2,1)} %bitcast.6, f32[1024,128]{1,0:T(8,128)} %bitcast.7, f32[1024,128]{1,0:T(8,128)} %bitcast.8, s32[1024,256]{1,0:T(8,128)} %list_ref.1, s32[8,128]{1,0:T(8,128)} %bitcast.9, s32[1024,256]{1,0:T(8,128)} %class_ref.1, bf16[2,1024,1024]{2,1,0:T(8,128)(2,1)} %state_ref.1), custom_call_target="tpu_custom_call" | custom-call | flops 2000000000 | bytes 20000000 | tf_op jit(solution)/shard_map/pallas_call | solution.py:326
  205.1 2.0 copy.9

commit v4 on v3

--- a/solution.py
+++ b/solution.py
@@ -10,18 +10,24 @@
 
 ITERS = 6
 MEMBERS = 128
-GROUP = 64
+PLANES = 8
+SITES = 8
+SHARE = 2
 LEVS = 4
 PER = 16
+AREA = PER * SITES
 QUART = PER // LEVS
 HALF = 128
 CAPACITY = 256
 LEVEL_OBS = 131072
 COLUMNS = 1024
-CHUNKS = 4
+CHUNKS = 8
 WIDE = COLUMNS // CHUNKS
 TILES = WIDE // 128
 GRAM_ROWS = MEMBERS + 8
+Z_ORDER = (1, 7, 2, 6, 3, 5, 4)
+X_ORDER = (1, 7, 2, 6, 3, 5, 4)
+EARLY = CHUNKS // 4
 
 MESH = pl.DeviceIdType.MESH
 HIGHEST = lax.Precision.HIGHEST
@@ -42,26 +48,37 @@
 def kernel(
     hx_ref, value_ref, error_ref, list_ref, count_ref, class_ref, state_ref,
     out_ref,
-    hx_in, hx_win, obs_in, pieces, slot_in, count_in, weight,
+    hx_plane, hx_in, hx_win, obs_in, pieces, slot_in, count_in, weight,
     gram_out, gram_in, upper, lower, mixers,
-    state_in, anomaly, product, result,
-    hx_send, hx_recv, halo_send, halo_recv, local_sem,
+    state_plane, state_in, anomaly, product, result, result_plane,
+    hx_z_send, hx_z_recv, hx_x_send, hx_x_recv, local_sem,
     gram_send, gram_recv, mix_send, mix_recv,
-    state_send, state_recv, out_send, out_recv,
+    state_z_send, state_z_recv, state_x_send, state_x_recv,
+    out_x_send, out_x_recv, out_z_send, out_z_recv,
 ):
     me = lax.axis_index("mem")
     lev = lax.axis_index("lev")
-    depth, low = me // 8, me % 8
-    before, after = (me + GROUP - 1) % GROUP, (me + 1) % GROUP
+    plane, site = lax.div(me, SITES), lax.rem(me, SITES)
+    before, after = lax.rem(me + 63, 64), lax.rem(me + 1, 64)
+
+    def along_z(step):
+        there = lax.rem(plane + step, PLANES)
+        return there, (there * SITES + site, lev)
+
+    def in_plane(step):
+        there = lax.rem(site + step, SITES)
+        return there, (plane * SITES + there, lev)
+
+    def greet(device):
+        pl.semaphore_signal(barrier, inc=1, device_id=device, device_id_type=MESH)
 
     barrier = pltpu.get_barrier_semaphore()
-
-    @pl.loop(1, GROUP)
-    def _(i):
-        pl.semaphore_signal(barrier, inc=1, device_id=((me + i) % GROUP, lev), device_id_type=MESH)
-
-    for i in range(1, LEVS):
-        pl.semaphore_signal(barrier, inc=1, device_id=(me, (lev + i) % LEVS), device_id_type=MESH)
+    for step in range(1, PLANES):
+        greet(along_z(step)[1])
+    for step in range(1, SITES):
+        greet(in_plane(step)[1])
+    for step in range(1, LEVS):
+        greet((me, lax.rem(lev + step, LEVS)))
 
     local = []
     for k, source in enumerate((value_ref, error_ref)):
@@ -79,57 +96,71 @@
     local.append(pltpu.make_async_copy(count_ref, count_in, local_sem.at[8]))
     for copy in local:
         copy.start()
-    pltpu.make_async_copy(
-        hx_ref.at[pl.ds(me * PER, PER)], hx_in.at[me], hx_recv
-    ).start()
     for q in range(CHUNKS):
-        cols = pl.ds(q * WIDE, WIDE)
         pltpu.make_async_copy(
-            state_ref.at[:, pl.ds(me * PER, PER), cols], state_in.at[q, pl.ds(me * 2, 2)], state_recv.at[q]
+            state_ref.at[:, pl.ds(plane * AREA, AREA), pl.ds(q * WIDE, WIDE)],
+            state_plane.at[q, pl.ds(plane * SHARE, SHARE)],
+            state_z_recv.at[q],
         ).start()
 
-    pl.semaphore_wait(barrier, GROUP - 1 + LEVS - 1)
-
-    def to_all(send):
-        @pl.loop(0, 8)
-        def _(j):
-            for dz in (4, 1, 7, 2, 6, 3, 5, 0):
-                target = ((depth + dz) % 8) * 8 + (low + j) % 8
-                if dz == 0:
-
-                    @pl.when(j > 0)
-                    def _():
-                        send(target)
-                else:
-                    send(target)
-
-    def send_hx(target):
+    def hx_pieces(there):
+        blocks = LEVEL_OBS // HALF
+        first = there * AREA
+        return (
+            (hx_ref.at[pl.ds(first, AREA)], hx_plane.at[plane, pl.ds(1, AREA)]),
+            (hx_ref.at[pl.ds(lax.rem(first + blocks - 1, blocks), 1)], hx_plane.at[plane, pl.ds(0, 1)]),
+            (hx_ref.at[pl.ds(lax.rem(first + AREA, blocks), 1)], hx_plane.at[plane, pl.ds(AREA + 1, 1)]),
+        )
+
+    for source, target in hx_pieces(plane):
+        pltpu.make_async_copy(source, target, hx_z_recv).start()
+
+    pl.semaphore_wait(barrier, PLANES - 1 + SITES - 1 + LEVS - 1)
+
+    def remote(source, target, send_sem, recv_sem, device):
         pltpu.make_async_remote_copy(
-            src_ref=hx_ref.at[pl.ds(target * PER, PER)],
-            dst_ref=hx_in.at[me],
-            send_sem=hx_send, recv_sem=hx_recv, device_id=(target, lev), device_id_type=MESH,
+            src_ref=source, dst_ref=target, send_sem=send_sem, recv_sem=recv_sem,
+            device_id=device, device_id_type=MESH,
         ).start()
 
-    to_all(send_hx)
+    for step in Z_ORDER:
+        there, device = along_z(step)
+        for source, target in hx_pieces(there):
+            remote(source, target, hx_z_send, hx_z_recv, device)
+
+    def send_state(q):
+        for step in Z_ORDER:
+            there, device = along_z(step)
+            remote(
+                state_ref.at[:, pl.ds(there * AREA, AREA), pl.ds(q * WIDE, WIDE)],
+                state_plane.at[q, pl.ds(plane * SHARE, SHARE)],
+                state_z_send, state_z_recv.at[q], device,
+            )
+
+    def pass_state(q):
+        pltpu.make_async_copy(state_plane.at[q], state_plane.at[q], state_z_recv.at[q]).wait()
+        for step in X_ORDER:
+            there, device = in_plane(step)
+            remote(
+                state_plane.at[q, :, pl.ds(there * PER, PER)],
+                state_in.at[q, pl.ds(site * 16, 16)],
+                state_x_send, state_x_recv.at[q], device,
+            )
+        pltpu.make_async_copy(
+            state_plane.at[q, :, pl.ds(site * PER, PER)],
+            state_in.at[q, pl.ds(site * 16, 16)],
+            state_x_recv.at[q],
+        ).start()
 
     for q in range(CHUNKS):
-
-        def send_state(target, q=q):
-            pltpu.make_async_remote_copy(
-                src_ref=state_ref.at[:, pl.ds(target * PER, PER), pl.ds(q * WIDE, WIDE)],
-                dst_ref=state_in.at[q, pl.ds(me * 2, 2)],
-                send_sem=state_send, recv_sem=state_recv.at[q],
-                device_id=(target, lev), device_id_type=MESH,
-            ).start()
-
-        to_all(send_state)
+        send_state(q)
 
     for copy in local:
         copy.wait()
     lanes = lax.broadcasted_iota(jnp.int32, (8, 128), 1)
     rows8 = lax.broadcasted_iota(jnp.int32, (8, 128), 0)
-    mine = jnp.sum(jnp.where(rows8 == me // 8, count_in[...], 0), axis=0, keepdims=True)
-    spots = lax.broadcasted_iota(jnp.int32, (PER, 128), 1) - (me % 8) * PER
+    mine = jnp.sum(jnp.where(rows8 == lax.div(me, 8), count_in[...], 0), axis=0, keepdims=True)
+    spots = lax.broadcasted_iota(jnp.int32, (PER, 128), 1) - lax.rem(me, 8) * PER
     patch_rows = lax.broadcasted_iota(jnp.int32, (PER, 128), 0)
     counts = jnp.sum(jnp.where(spots == patch_rows, mine, 0), axis=1, keepdims=True)
     slots = lax.broadcasted_iota(jnp.int32, (PER, CAPACITY), 1)
@@ -143,27 +174,18 @@
             pieces[k * 3 + j] = piece
             rest = rest - piece
 
-    pltpu.make_async_copy(hx_in, hx_in, hx_recv).wait()
-
-    def take_block(b):
-        hx_win[b + 1] = hx_in[:, b].astype(f32).reshape(MEMBERS, 128).astype(bf16)
-
-    for b in range(PER):
-        take_block(b)
-    halo = [
-        pltpu.make_async_remote_copy(
-            src_ref=hx_win.at[1], dst_ref=hx_win.at[PER + 1],
-            send_sem=halo_send.at[0], recv_sem=halo_recv.at[0],
-            device_id=(before, lev), device_id_type=MESH,
-        ),
-        pltpu.make_async_remote_copy(
-            src_ref=hx_win.at[PER], dst_ref=hx_win.at[0],
-            send_sem=halo_send.at[1], recv_sem=halo_recv.at[1],
-            device_id=(after, lev), device_id_type=MESH,
-        ),
-    ]
-    for copy in halo:
-        copy.start()
+    pltpu.make_async_copy(hx_plane, hx_plane, hx_z_recv).wait()
+    for step in X_ORDER:
+        there, device = in_plane(step)
+        remote(
+            hx_plane.at[:, pl.ds(there * PER, PER + 2)], hx_in.at[site], hx_x_send, hx_x_recv, device
+        )
+    pltpu.make_async_copy(
+        hx_plane.at[:, pl.ds(site * PER, PER + 2)], hx_in.at[site], hx_x_recv
+    ).start()
+    pltpu.make_async_copy(hx_in, hx_in, hx_x_recv).wait()
+    for b in range(PER + 2):
+        hx_win[b] = hx_in[:, :, b].astype(f32).reshape(MEMBERS, 128).astype(bf16)
 
     def patch_gram(p):
         anchor = (me * PER + p - 1) * HALF
@@ -185,20 +207,13 @@
         both = jnp.concatenate([spread, jnp.broadcast_to(average, (8, CAPACITY))], axis=0)
         gram_out[p] = dot_nt(both, spread, HIGHEST)
 
-    @pl.loop(1, PER - 1)
+    @pl.loop(0, PER)
     def _(p):
         patch_gram(p)
 
-    for copy in halo:
-        copy.wait()
-
-    @pl.loop(0, 2)
-    def _(i):
-        patch_gram(i * (PER - 1))
-
     gram_copies = []
     for i in range(1, LEVS):
-        target = (lev + i) % LEVS
+        target = lax.rem(lev + i, LEVS)
         gram_copies.append(
             pltpu.make_async_remote_copy(
                 src_ref=gram_out.at[pl.ds(target * QUART, QUART)],
@@ -209,6 +224,8 @@
         )
     for copy in gram_copies:
         copy.start()
+    for q in range(EARLY):
+        pass_state(q)
     for copy in gram_copies:
         copy.wait()
 
@@ -247,7 +264,7 @@
 
     mix_copies = []
     for i in range(1, LEVS):
-        target = (lev + i) % LEVS
+        target = lax.rem(lev + i, LEVS)
         mix_copies.append(
             pltpu.make_async_remote_copy(
                 src_ref=mixers.at[pl.ds(lev * QUART, QUART)],
@@ -258,12 +275,13 @@
         )
     for copy in mix_copies:
         copy.start()
+    for q in range(EARLY, 2 * EARLY):
+        pass_state(q)
     for copy in mix_copies:
         copy.wait()
 
-    for q in range(CHUNKS):
-        cols = pl.ds(q * WIDE, WIDE)
-        pltpu.make_async_copy(state_in.at[q], state_in.at[q], state_recv.at[q]).wait()
+    def apply(q):
+        pltpu.make_async_copy(state_in.at[q], state_in.at[q], state_x_recv.at[q]).wait()
         for t in range(TILES):
             tile = slice(t * 128, (t + 1) * 128)
 
@@ -295,28 +313,51 @@
                 block = product[t, pl.ds(i * 8 * PER, 8 * PER), :]
                 result[q, pl.ds(i * 8, 8), :, tile] = block.reshape(8, PER, 128).astype(bf16)
 
+        for step in X_ORDER:
+            there, device = in_plane(step)
+            remote(
+                result.at[q, pl.ds(there * 16, 16)],
+                result_plane.at[q, :, pl.ds(site * PER, PER)],
+                out_x_send, out_x_recv.at[q], device,
+            )
         pltpu.make_async_copy(
-            result.at[q, pl.ds(me * 2, 2)], out_ref.at[:, pl.ds(me * PER, PER), cols], out_recv
+            result.at[q, pl.ds(site * 16, 16)],
+            result_plane.at[q, :, pl.ds(site * PER, PER)],
+            out_x_recv.at[q],
         ).start()
 
-        def send_result(target, q=q, cols=cols):
-            pltpu.make_async_remote_copy(
-                src_ref=result.at[q, pl.ds(target * 2, 2)],
-                dst_ref=out_ref.at[:, pl.ds(me * PER, PER), cols],
-                send_sem=out_send, recv_sem=out_recv,
-                device_id=(target, lev), device_id_type=MESH,
-            ).start()
-
-        to_all(send_result)
-
-    others = GROUP - 1
-    pltpu.make_async_copy(
-        hx_in.at[pl.ds(0, others)], hx_in.at[pl.ds(0, others)], hx_send
-    ).wait()
-    sent = state_ref.at[:, pl.ds(0, PER * others)]
-    pltpu.make_async_copy(sent, sent, state_send).wait()
-    pltpu.make_async_copy(sent, sent, out_send).wait()
-    pltpu.make_async_copy(out_ref, out_ref, out_recv).wait()
+    def pass_result(q):
+        cols = pl.ds(q * WIDE, WIDE)
+        pltpu.make_async_copy(result_plane.at[q], result_plane.at[q], out_x_recv.at[q]).wait()
+        for step in Z_ORDER:
+            there, device = along_z(step)
+            remote(
+                result_plane.at[q, pl.ds(there * SHARE, SHARE)],
+                out_ref.at[:, pl.ds(plane * AREA, AREA), cols],
+                out_z_send, out_z_recv, device,
+            )
+        pltpu.make_async_copy(
+            result_plane.at[q, pl.ds(plane * SHARE, SHARE)],
+            out_ref.at[:, pl.ds(plane * AREA, AREA), cols],
+            out_z_recv,
+        ).start()
+
+    for q in range(CHUNKS):
+        apply(q)
+        if q + 2 * EARLY < CHUNKS:
+            pass_state(q + 2 * EARLY)
+        if q >= 1:
+            pass_result(q - 1)
+    pass_result(CHUNKS - 1)
+
+    others = hx_plane.at[pl.ds(0, PLANES - 1)]
+    pltpu.make_async_copy(others, others, hx_z_send).wait()
+    others = hx_in.at[pl.ds(0, SITES - 1)]
+    pltpu.make_async_copy(others, others, hx_x_send).wait()
+    others = state_ref.at[:, pl.ds(0, AREA * (PLANES - 1))]
+    for sem in (state_z_send, state_x_send, out_x_send, out_z_send):
+        pltpu.make_async_copy(others, others, sem).wait()
+    pltpu.make_async_copy(out_ref, out_ref, out_z_recv).wait()
 
 
 def body(hx_ens, obs_value, obs_error, obs_list, obs_count, loc_class, state):
@@ -329,7 +370,8 @@
         in_specs=[any_space] * 7,
         out_specs=pl.BlockSpec(memory_space=pltpu.VMEM),
         scratch_shapes=[
-            pltpu.VMEM((GROUP, PER, 2, 128), bf16),
+            pltpu.VMEM((PLANES, AREA + 2, SHARE, 128), bf16),
+            pltpu.VMEM((SITES, PLANES, PER + 2, SHARE, 128), bf16),
             pltpu.VMEM((PER + 2, MEMBERS, 128), bf16),
             pltpu.VMEM((2, 3 * PER, 128), f32),
             pltpu.VMEM((6, 3 * PER, 128), f32),
@@ -341,12 +383,15 @@
             pltpu.VMEM((QUART, MEMBERS, MEMBERS), f32),
             pltpu.VMEM((QUART, MEMBERS, MEMBERS), f32),
             pltpu.VMEM((PER, MEMBERS, MEMBERS), bf16),
+            pltpu.VMEM((CHUNKS, 16, AREA, WIDE), bf16),
             pltpu.VMEM((CHUNKS, MEMBERS, PER, WIDE), bf16),
             pltpu.VMEM((TILES, MEMBERS * PER, 128), f32),
             pltpu.VMEM((TILES, MEMBERS * PER, 128), f32),
             pltpu.VMEM((CHUNKS, MEMBERS, PER, WIDE), bf16),
-            dma, dma, dma((2,)), dma((2,)), dma((9,)),
+            pltpu.VMEM((CHUNKS, 16, AREA, WIDE), bf16),
+            dma, dma, dma, dma, dma((9,)),
             dma((3,)), dma((3,)), dma((3,)), dma((3,)),
+            dma, dma((CHUNKS,)), dma, dma((CHUNKS,)),
             dma, dma((CHUNKS,)), dma, dma,
         ],
         compiler_params=pltpu.CompilerParams(

time: 207 us -> 204 us (0.986)
  Pallas kernels: 205 us -> 201 us
    pallas_call x1, Pallas kernels: 205 us -> 201 us  [body(): pl.pallas_call(kernel, out_shape=pltpu.VMEM(state.shape, bf16), in_specs=...]
where the time goes in v4:
time: 204 us; the launch traced here: 203 us
  Pallas kernels  201 us (99%)
    pallas_call x1, Pallas kernels, body(): pl.pallas_call(kernel, out_shape=pltpu.VMEM(state.shape, bf16), in_specs=...  201 us

profile of v4, /device:TPU:1, one launch (start us, length us, event | category | flops | bytes accessed | tf_op | source)
XLA Modules:
  0.0 203.4 jit_solution(3886419983091487035)
XLA Ops:
  0.0 201.4 %shard_map.73 = bf16[2,1024,1024]{2,1,0:T(8,128)(2,1)S(1)} custom-call(bf16[1024,2,128]{2,1,0:T(2,128)(2,1)} %bitcast.6, f32[1024,128]{1,0:T(8,128)} %bitcast.7, f32[1024,128]{1,0:T(8,128)} %bitcast.8, s32[1024,256]{1,0:T(8,128)} %list_ref.1, s32[8,128]{1,0:T(8,128)} %bitcast.9, s32[1024,256]{1,0:T(8,128)} %class_ref.1, bf16[2,1024,1024]{2,1,0:T(8,128)(2,1)} %state_ref.1), custom_call_target="tpu_custom_call" | custom-call | flops 2000000000 | bytes 20000000 | tf_op jit(solution)/shard_map/pallas_call | solution.py:367
  201.4 2.0 copy.9

commit v5 on v4

--- a/solution.py
+++ b/solution.py
@@ -344,10 +344,10 @@
 
     for q in range(CHUNKS):
         apply(q)
+        if q >= 1:
+            pass_result(q - 1)
         if q + 2 * EARLY < CHUNKS:
             pass_state(q + 2 * EARLY)
-        if q >= 1:
-            pass_result(q - 1)
     pass_result(CHUNKS - 1)
 
     others = hx_plane.at[pl.ds(0, PLANES - 1)]

time: 204 us -> 204 us (level)
  no operation moved by 1% of the time
where the time goes in v5:
time: 204 us; the launch traced here: 203 us
  Pallas kernels  201 us (99%)
    pallas_call x1, Pallas kernels, body(): pl.pallas_call(kernel, out_shape=pltpu.VMEM(state.shape, bf16), in_specs=...  201 us

profile of v5, /device:TPU:1, one launch (start us, length us, event | category | flops | bytes accessed | tf_op | source)
XLA Modules:
  0.0 203.4 jit_solution(12226155358652812822)
XLA Ops:
  0.0 201.4 %shard_map.73 = bf16[2,1024,1024]{2,1,0:T(8,128)(2,1)S(1)} custom-call(bf16[1024,2,128]{2,1,0:T(2,128)(2,1)} %bitcast.6, f32[1024,128]{1,0:T(8,128)} %bitcast.7, f32[1024,128]{1,0:T(8,128)} %bitcast.8, s32[1024,256]{1,0:T(8,128)} %list_ref.1, s32[8,128]{1,0:T(8,128)} %bitcast.9, s32[1024,256]{1,0:T(8,128)} %class_ref.1, bf16[2,1024,1024]{2,1,0:T(8,128)(2,1)} %state_ref.1), custom_call_target="tpu_custom_call" | custom-call | flops 2000000000 | bytes 20000000 | tf_op jit(solution)/shard_map/pallas_call | solution.py:367
  201.4 2.0 copy.9
